TPU v7x, 512 devices: a whole 4x4x16 slice. The times are simulated.
512 devices in a mesh: row: 16 (over y, z_hi), col: 32 (over x, z_lo, core).
Axes of the slice: x: 4, y: 4, z: 16 (z_hi: 4, z_lo: 4; z = z_hi * 4 + z_lo), core: 2. Of those that a mesh axis runs over, the one named last changes fastest.
Arguments:
- positions: float32 [3, 524288], P(None, ('row', 'col')), may hold values from 0 to 1
- strengths: float32 [3, 524288], P(None, ('row', 'col')), may hold values from -0.06 to 0.06
- radii: float32 [524288], P(('row', 'col')), may hold values from 0.1 to 0.3
- pair_list: int32 [2, 16, 32, 2], P(None, 'row', 'col'), may hold values from 0 to 31, as said below
- pair_count: int32 [16, 32], P('row', 'col'), may hold values from 1 to 2, as said below
Outputs:
- velocity: float32 [3, 524288], P(None, ('row', 'col'))
- stretching: float32 [3, 524288], P(None, ('row', 'col'))
Inputs may be any that keep to these rules, and one draw needn't show every extreme that they name: `pair_list`: row-block indices lie in 0 to 31, column-block indices in 0 to 15; slot 0 of every tile pairs a group with itself. `pair_count`: some tile fills all 2 slots.
All inputs are finite; a program needn't handle non-finite values.
Results may differ from a plain program's by a relative error of at most 0.0003.
Values sent between devices are 32-bit elements; how exact they have to be, the bound alone decides.
A program may use at most 192 MiB of HBM per device.

v0:
```python
import jax
import jax.numpy as jnp
from jax import lax
from jax.sharding import PartitionSpec as P

G = 1024
GD = 1


def cross_rows(u_a, u_b):
    return jnp.stack(
        [
            u_a[1] * u_b[2] - u_a[2] * u_b[1],
            u_a[2] * u_b[0] - u_a[0] * u_b[2],
            u_a[0] * u_b[1] - u_a[1] * u_b[0],
        ]
    )


def pair_terms(pos_a, str_a, rad_a, pos_b, str_b, rad_b):
    rvec = pos_a[:, :, None] - pos_b[:, None, :]
    rho = jnp.sum(rvec * rvec, axis=0)
    spread = 0.5 * (rad_a[:, None] ** 2 + rad_b[None, :] ** 2)
    inner = rho + spread
    power = inner ** (-2.5)
    upper = rho + 2.5 * spread
    kern = upper * power
    slope = 2.0 * (power - 2.5 * upper * power / inner)
    scale = 1.0 / (4.0 * jnp.pi)
    sa = str_a[:, :, None]
    sb = str_b[:, None, :]
    r_x_b = cross_rows(rvec, sb)
    r_x_a = cross_rows(rvec, sa)
    a_x_b = cross_rows(sa, sb)
    dot_a = jnp.sum(sa * rvec, axis=0)
    dot_b = jnp.sum(sb * rvec, axis=0)
    vel_a = -scale * jnp.sum(kern * r_x_b, axis=2)
    vel_b = scale * jnp.sum(kern * r_x_a, axis=1)
    str_ta = -scale * jnp.sum(kern * a_x_b + slope * dot_a * r_x_b, axis=2)
    str_tb = -scale * jnp.sum(-kern * a_x_b + slope * dot_b * r_x_a, axis=1)
    return (jnp.concatenate([vel_a, str_ta]), jnp.concatenate([vel_b, str_tb]))


def local(positions, strengths, radii, pair_list, pair_count):
    row_pos, row_str, row_rad = (
        lax.all_gather(positions, "col", axis=1, tiled=True),
        lax.all_gather(strengths, "col", axis=1, tiled=True),
        lax.all_gather(radii, "col", axis=0, tiled=True),
    )
    col_pos, col_str, col_rad = (
        lax.all_gather(positions, "row", axis=1, tiled=True),
        lax.all_gather(strengths, "row", axis=1, tiled=True),
        lax.all_gather(radii, "row", axis=0, tiled=True),
    )
    row_here = lax.axis_index("row")
    col_here = lax.axis_index("col")
    listed = pair_list[:, 0, 0, :]
    count = pair_count[0, 0]
    row_acc = jnp.zeros((6, row_pos.shape[1]), jnp.float32)
    col_acc = jnp.zeros((6, col_pos.shape[1]), jnp.float32)

    def visit(slot, accs):
        acc_row, acc_col = accs
        kk = listed[0, slot]
        mm = listed[1, slot]
        sa = kk * G
        sb = mm * G
        pa = lax.dynamic_slice_in_dim(row_pos, sa, G, 1)
        ta = lax.dynamic_slice_in_dim(row_str, sa, G, 1)
        ra = lax.dynamic_slice_in_dim(row_rad, sa, G, 0)
        pb = lax.dynamic_slice_in_dim(col_pos, sb, G, 1)
        tb = lax.dynamic_slice_in_dim(col_str, sb, G, 1)
        rb = lax.dynamic_slice_in_dim(col_rad, sb, G, 0)
        side_a, side_b = pair_terms(pa, ta, ra, pb, tb, rb)
        same = (kk // GD == col_here) & (mm // GD == row_here) & (kk % GD == mm % GD)
        live = jnp.where(slot < count, 1.0, 0.0).astype(jnp.float32)
        other = live * jnp.where(same, 0.0, 1.0).astype(jnp.float32)
        cur_a = lax.dynamic_slice_in_dim(acc_row, sa, G, 1)
        acc_row = lax.dynamic_update_slice_in_dim(acc_row, cur_a + live * side_a, sa, 1)
        cur_b = lax.dynamic_slice_in_dim(acc_col, sb, G, 1)
        acc_col = lax.dynamic_update_slice_in_dim(acc_col, cur_b + other * side_b, sb, 1)
        return (acc_row, acc_col)

    row_acc, col_acc = lax.fori_loop(0, listed.shape[1], visit, (row_acc, col_acc))
    row_part = lax.psum_scatter(row_acc, "col", scatter_dimension=1, tiled=True)
    col_part = lax.psum_scatter(col_acc, "row", scatter_dimension=1, tiled=True)
    total = row_part + col_part
    return (total[:3], total[3:])


def solution(mesh):
    placed = (
        P(None, ("row", "col")),
        P(None, ("row", "col")),
        P(("row", "col")),
        P(None, "row", "col", None),
        P("row", "col"),
    )
    return jax.shard_map(
        local,
        mesh=mesh,
        in_specs=placed,
        out_specs=(P(None, ("row", "col")), P(None, ("row", "col"))),
        check_vma=False,
    )
```

profile of v0, /device:TPU:1, one launch (start us, length us, event | category | flops | bytes accessed | tf_op | source)
XLA Modules:
  0.0 688.8 jit_solution(8325875045078800553)
XLA Ops:
  7.2 0.0 reduce-scatter.5.cloned.1.call-start
  7.2 50.9 %all_gather.18 = f32[3,32768]{1,0:T(4,128)} all-gather(f32[3,1024]{1,0:T(4,128)} %param.7), channel_id=1, replica_groups=mesh['row'=16,'col'=32] {'col'}, dimensions={1}, use_global_device_ids=true | all-gather | bytes 405504 | tf_op jit(solution)/shard_map/all_gather | solution.py:46
  58.1 52.8 %all_gather.19 = f32[3,16384]{1,0:T(4,128)} all-gather(f32[3,1024]{1,0:T(4,128)} %param.7), channel_id=1, replica_groups=mesh['row'=16,'col'=32] {'row'}, dimensions={1}, use_global_device_ids=true | all-gather | bytes 208896 | tf_op jit(solution)/shard_map/all_gather | solution.py:51
  110.9 45.2 %all_gather.20 = f32[32768]{0:T(1024)S(1)} all-gather(f32[1024]{0:T(1024)} %param.9), channel_id=1, replica_groups=mesh['row'=16,'col'=32] {'col'}, dimensions={0}, use_global_device_ids=true | all-gather | bytes 135168 | tf_op jit(solution)/shard_map/all_gather | solution.py:48
  156.1 42.4 %all_gather.21 = f32[16384]{0:T(1024)} all-gather(f32[1024]{0:T(1024)} %param.9), channel_id=1, replica_groups=mesh['row'=16,'col'=32] {'row'}, dimensions={0}, use_global_device_ids=true | all-gather | bytes 69632 | tf_op jit(solution)/shard_map/all_gather | solution.py:53
  198.5 44.5 %all_gather.22 = f32[3,16384]{1,0:T(4,128)S(1)} all-gather(f32[3,1024]{1,0:T(4,128)} %param.8), channel_id=1, replica_groups=mesh['row'=16,'col'=32] {'row'}, dimensions={1}, use_global_device_ids=true | all-gather | bytes 208896 | tf_op jit(solution)/shard_map/all_gather | solution.py:52
  242.9 58.6 %all_gather.23 = f32[3,32768]{1,0:T(4,128)} all-gather(f32[3,1024]{1,0:T(4,128)} %param.8), channel_id=1, replica_groups=mesh['row'=16,'col'=32] {'col'}, dimensions={1}, use_global_device_ids=true | all-gather | bytes 405504 | tf_op jit(solution)/shard_map/all_gather | solution.py:47
  301.6 1.1 broadcast_in_dim.38
  302.7 133.0 %while.18 = (s32[]{:T(128)}, f32[6,32768]{1,0:T(8,128)}, f32[6,16384]{1,0:T(8,128)S(1)}, s32[2,2]{1,0:T(2,128)}, s32[]{:T(128)}, /*index=5*/f32[3,32768]{1,0:T(4...) while((s32[]{:T(128)}, f32[6,32768]{1,0:T(8,128)}, ...), condition=%wide.region_8.9_spmd, body=%wide.region_0.8_spmd.sunk | while | flops 118528008 | bytes 227082864 | solution.py:84
  302.7 1.4 constant_dynamic-slice_fusion.13
  305.3 0.7 constant_dynamic-slice_fusion.15
  306.0 0.7 constant_dynamic-slice_fusion.16
  306.8 0.7 constant_dynamic-slice_fusion.17
  307.5 11.8 %fusion.20 = (f32[1024,1024]{1,0:T(8,128)}, f32[1024,1024]{1,0:T(8,128)}, f32[1024,1024]{1,0:T(8,128)}, f32[3,1024,1024]{2,1,0:T(8,128)}) fusion(f32[3,1024]{1,0:T(4,128)S(1)} %constant_dynamic-slice_fusion.14, f32[3,1024]{1,0:T(4,128)S(1)} %constant_dynamic-slice_fusion.15, f32[3,1024]{1,0:T(4,128)S(1)} %constant_dynamic-slice_fusion.16, ...), kind=kLoop, calls=%fused_computation.5.clone.1 | loop fusion | flops 18874368 | bytes 25214976 | tf_op jit(solution)/shard_map/while/body/eval_jaxpr/reduce_sum | solution.py:36
  319.3 0.9 fusion.21
  320.2 0.1 fusion.22
  320.3 17.5 %multiply_subtract_fusion.10 = (f32[1,1024,1024]{2,1,0:T(8,128)}, f32[1,1024,1024]{2,1,0:T(8,128)}, f32[1,1024,1024]{2,1,0:T(8,128)}, f32[1,1024,1024]{2,1,0:T(8...) fusion(f32[3,1024,1024]{2,1,0:T(8,128)} %get-tuple-element.533,, ...), kind=kLoop, calls=%fused_computation.20.clone.1 | loop fusion | flops 28311552 | bytes 50356224 | tf_op jit(solution)/shard_map/while/body/eval_jaxpr/sub | solution.py:13
  337.9 0.7 dynamic-slice_multiply_fusion.4
  338.5 0.0 copy-done
  338.5 0.0 copy-start.2
  338.5 0.0 copy-start.3
  338.6 11.7 %fusion.23 = (f32[1024,1024]{1,0:T(8,128)}, f32[1024,1024]{1,0:T(8,128)}, f32[1024,1024]{1,0:T(8,128)}, f32[1024,1024]{1,0:T(8,128)}) fusion(f32[1024,1024]{1,0:T(8,128)} %get-tuple-element.543, f32[1024]{0:T(1024)S(1)} %dynamic-slice_multiply_fusion.4, f32[1024]{0:T(1024)S(1)} %dynamic-slice_multiply_fusion.5, f32[1024,1024]{1,0:T(8,128)S(1)} %copy-done, ...), kind=kLoop, calls=%fused_computation.51.clone.1 | loop fusion | flops 14680064 | bytes 29368320 | tf_op jit(solution)/shard_map/while/body/eval_jaxpr/neg | solution.py:40
  350.3 0.0 copy-done.1
  350.3 0.0 copy-done.2
  350.3 0.3 copy-done.3
  350.6 15.3 %multiply_reduce_fusion.3 = (f32[3,1024]{1,0:T(4,128)S(1)}, f32[3,1024]{1,0:T(4,128)S(1)}, f32[3,1024]{1,0:T(4,128)S(1)}, f32[3,1024]{1,0:T(4,128)S(1)}) fusion(f32[1,1024,1024]{2,1,0:T(8,128)} %get-tuple-element.540, f32[1,1024,1024]{2,1,0:T(8,128)} %get-tuple-element.541, f32[1,1024,1024]{2,1,0:T(8,128)} %get-tuple-element.542, ...), kind=kLoop, calls=%fused_computation.12.clone.1 | loop fusion | flops 56610816 | bytes 54575104 | tf_op jit(solution)/shard_map/while/body/eval_jaxpr/reduce_sum | solution.py:37
  367.8 1.4 fusion.24
  369.2 1.4 constant_dynamic-slice_fusion.13
  371.8 0.7 constant_dynamic-slice_fusion.15
  372.5 0.7 constant_dynamic-slice_fusion.16
  373.2 0.7 constant_dynamic-slice_fusion.17
  374.0 11.8 %fusion.20 = (f32[1024,1024]{1,0:T(8,128)}, f32[1024,1024]{1,0:T(8,128)}, f32[1024,1024]{1,0:T(8,128)}, f32[3,1024,1024]{2,1,0:T(8,128)}) fusion(f32[3,1024]{1,0:T(4,128)S(1)} %constant_dynamic-slice_fusion.14, f32[3,1024]{1,0:T(4,128)S(1)} %constant_dynamic-slice_fusion.15, f32[3,1024]{1,0:T(4,128)S(1)} %constant_dynamic-slice_fusion.16, ...), kind=kLoop, calls=%fused_computation.5.clone.1 | loop fusion | flops 18874368 | bytes 25214976 | tf_op jit(solution)/shard_map/while/body/eval_jaxpr/reduce_sum | solution.py:36
  385.8 0.9 fusion.21
  386.7 0.1 fusion.22
  386.8 17.5 %multiply_subtract_fusion.10 = (f32[1,1024,1024]{2,1,0:T(8,128)}, f32[1,1024,1024]{2,1,0:T(8,128)}, f32[1,1024,1024]{2,1,0:T(8,128)}, f32[1,1024,1024]{2,1,0:T(8...) fusion(f32[3,1024,1024]{2,1,0:T(8,128)} %get-tuple-element.533,, ...), kind=kLoop, calls=%fused_computation.20.clone.1 | loop fusion | flops 28311552 | bytes 50356224 | tf_op jit(solution)/shard_map/while/body/eval_jaxpr/sub | solution.py:13
  404.3 0.7 dynamic-slice_multiply_fusion.4
  405.0 11.7 %fusion.23 = (f32[1024,1024]{1,0:T(8,128)}, f32[1024,1024]{1,0:T(8,128)}, f32[1024,1024]{1,0:T(8,128)}, f32[1024,1024]{1,0:T(8,128)}) fusion(f32[1024,1024]{1,0:T(8,128)} %get-tuple-element.543, f32[1024]{0:T(1024)S(1)} %dynamic-slice_multiply_fusion.4, f32[1024]{0:T(1024)S(1)} %dynamic-slice_multiply_fusion.5, f32[1024,1024]{1,0:T(8,128)S(1)} %copy-done, ...), kind=kLoop, calls=%fused_computation.51.clone.1 | loop fusion | flops 14680064 | bytes 29368320 | tf_op jit(solution)/shard_map/while/body/eval_jaxpr/neg | solution.py:40
  416.8 0.3 copy-done.3
  417.1 15.3 %multiply_reduce_fusion.3 = (f32[3,1024]{1,0:T(4,128)S(1)}, f32[3,1024]{1,0:T(4,128)S(1)}, f32[3,1024]{1,0:T(4,128)S(1)}, f32[3,1024]{1,0:T(4,128)S(1)}) fusion(f32[1,1024,1024]{2,1,0:T(8,128)} %get-tuple-element.540, f32[1,1024,1024]{2,1,0:T(8,128)} %get-tuple-element.541, f32[1,1024,1024]{2,1,0:T(8,128)} %get-tuple-element.542, ...), kind=kLoop, calls=%fused_computation.12.clone.1 | loop fusion | flops 56610816 | bytes 54575104 | tf_op jit(solution)/shard_map/while/body/eval_jaxpr/reduce_sum | solution.py:37
  434.3 1.4 fusion.24
  435.7 0.8 copy-done.4
  436.4 0.0 reduce-scatter.5.cloned.1.call-update
  436.5 0.0 reduce-scatter.3.cloned.1.call-start
  436.5 0.7 reduce-scatter.3.cloned.1.call-update
  437.2 98.4 %reduce-scatter.5.cloned.1.call-done = f32[6,1024]{1,0:T(8,128)} async-done(((f32[6,16384]{1,0:T(8,128)}), f32[6,1024]{1,0:T(8,128)}) %reduce-scatter.5.cloned.1.call-update) | async-done | bytes 24592 | tf_op jit(solution)/shard_map/reduce_scatter | solution.py:86
  535.6 144.9 %reduce-scatter.3.cloned.1.call-done = f32[6,1024]{1,0:T(8,128)} async-done(((f32[6,32768]{1,0:T(8,128)}), f32[6,1024]{1,0:T(8,128)}) %reduce-scatter.3.cloned.1.call-update) | async-done | bytes 24592 | tf_op jit(solution)/shard_map/reduce_scatter | solution.py:85
  680.6 0.8 add.280
  681.3 0.6 fusion.14
  (23 shorter events, 0.1 us)
Async XLA Ops:
  7.2 528.5 %reduce-scatter.5.cloned.1.call-start = ((), (), s32[]{:S(2)}) async-start(), calls=%async_computation.3 | async-start | bytes 557056 | tf_op jit(solution)/shard_map/reduce_scatter | solution.py:86
  320.3 18.2 %copy-start = (f32[1024,1024]{1,0:T(8,128)S(1)}, f32[1024,1024]{1,0:T(8,128)}, u32[]{:S(2)}) copy-start(f32[1024,1024]{1,0:T(8,128)} %get-tuple-element.544) | copy-start | bytes 12582916 | tf_op jit(solution)/shard_map/while
  338.5 11.7 %copy-start.1 = (f32[1,1024,1024]{2,1,0:T(8,128)S(1)}, f32[1,1024,1024]{2,1,0:T(8,128)}, u32[]{:S(2)}) copy-start(f32[1,1024,1024]{2,1,0:T(8,128)} %get-tuple-element.553) | copy-start | bytes 12582916 | tf_op jit(solution)/shard_map/while
  338.5 11.7 %copy-start.2 = (f32[1,1024,1024]{2,1,0:T(8,128)S(1)}, f32[1,1024,1024]{2,1,0:T(8,128)}, u32[]{:S(2)}) copy-start(f32[1,1024,1024]{2,1,0:T(8,128)} %get-tuple-element.552) | copy-start | bytes 12582916 | tf_op jit(solution)/shard_map/while
  338.5 12.1 %copy-start.3 = (f32[1,1024,1024]{2,1,0:T(8,128)S(1)}, f32[1,1024,1024]{2,1,0:T(8,128)}, u32[]{:S(2)}) copy-start(f32[1,1024,1024]{2,1,0:T(8,128)} %get-tuple-element.551) | copy-start | bytes 12582916 | tf_op jit(solution)/shard_map/while
  386.8 18.2 %copy-start = (f32[1024,1024]{1,0:T(8,128)S(1)}, f32[1024,1024]{1,0:T(8,128)}, u32[]{:S(2)}) copy-start(f32[1024,1024]{1,0:T(8,128)} %get-tuple-element.544) | copy-start | bytes 12582916 | tf_op jit(solution)/shard_map/while
  405.0 11.7 %copy-start.1 = (f32[1,1024,1024]{2,1,0:T(8,128)S(1)}, f32[1,1024,1024]{2,1,0:T(8,128)}, u32[]{:S(2)}) copy-start(f32[1,1024,1024]{2,1,0:T(8,128)} %get-tuple-element.553) | copy-start | bytes 12582916 | tf_op jit(solution)/shard_map/while
  405.0 11.7 %copy-start.2 = (f32[1,1024,1024]{2,1,0:T(8,128)S(1)}, f32[1,1024,1024]{2,1,0:T(8,128)}, u32[]{:S(2)}) copy-start(f32[1,1024,1024]{2,1,0:T(8,128)} %get-tuple-element.552) | copy-start | bytes 12582916 | tf_op jit(solution)/shard_map/while
  405.0 12.1 %copy-start.3 = (f32[1,1024,1024]{2,1,0:T(8,128)S(1)}, f32[1,1024,1024]{2,1,0:T(8,128)}, u32[]{:S(2)}) copy-start(f32[1,1024,1024]{2,1,0:T(8,128)} %get-tuple-element.551) | copy-start | bytes 12582916 | tf_op jit(solution)/shard_map/while
  435.7 0.8 copy-start.4
  436.5 244.1 %reduce-scatter.3.cloned.1.call-start = ((), (), s32[]{:S(2)}) async-start(), calls=%async_computation.2 | async-start | bytes 1081344 | tf_op jit(solution)/shard_map/reduce_scatter | solution.py:85
Sparse Core Ops, SparseCore 0:
  436.6 99.0 reduce-scatter.4
  538.7 141.8 reduce-scatter.2
where the time goes:
time: 694 us; the launch traced here: 689 us
  blocking collectives  294 us (42%)
  waiting for transfers between devices  244 us (35%)
  other arithmetic  118 us (17%)
  between operations  14 us (2%)
  local copies, waits for them, and re-layouts  12.3 us (2%)
    reduce_scatter x1, waiting for transfers between devices, local(): row_part = lax.psum_scatter(row_acc, 'col', scatter_dimension=1, tiled=True)  145 us
    reduce_scatter x1, waiting for transfers between devices, local(): col_part = lax.psum_scatter(col_acc, 'row', scatter_dimension=1, tiled=True)  98.4 us
    all_gather x1, blocking collectives, local(): lax.all_gather(strengths, 'col', axis=1, tiled=True)  58.6 us
    all_gather x1, blocking collectives, local(): lax.all_gather(positions, 'row', axis=1, tiled=True)  52.8 us
    all_gather x1, blocking collectives, local(): lax.all_gather(positions, 'col', axis=1, tiled=True)  50.9 us
    all_gather x1, blocking collectives, local(): lax.all_gather(radii, 'col', axis=0, tiled=True)  45.2 us
    all_gather x1, blocking collectives, local(): lax.all_gather(strengths, 'row', axis=1, tiled=True)  44.5 us
    all_gather x1, blocking collectives, local(): lax.all_gather(radii, 'row', axis=0, tiled=True)  42.4 us
  transfers between devices with their start and end apart: 2, of which 2 were waited for; matrix products, arithmetic and copies ran while one was open for 0% of the time, Pallas kernels for 0%

commit v1 on v0

v1 whole, which is shorter than its diff:
```python
import functools
import math

import jax
import jax.numpy as jnp
from jax import lax
from jax.experimental import pallas as pl
from jax.experimental.pallas import tpu as pltpu
from jax.sharding import PartitionSpec as P

G = 1024
MESH = pl.DeviceIdType.MESH
f32, bf16 = jnp.float32, jnp.bfloat16
TI, TJ = 512, 256

NY, NH, NX, NL, NC = 4, 4, 4, 4, 2
NEAR = [(dx, dc) for dx in range(NX) for dc in range(NC)]


def coords():
    r, c = lax.axis_index("row"), lax.axis_index("col")
    return r // NH, r % NH, c // (NL * NC), (c // NC) % NL, c % NC


def at(dy=0, dh=0, dx=0, dl=0, dc=0):
    y, h, x, l, c = coords()
    row = ((y + dy) % NY) * NH + (h + dh) % NH
    col = (((x + dx) % NX) * NL + (l + dl) % NL) * NC + (c + dc) % NC
    return {"row": row, "col": col}


def split3(v):
    h = v.astype(bf16).astype(f32)
    rest = v - h
    m = rest.astype(bf16).astype(f32)
    return h, m, rest - m


def cross(p, q):
    return [p[1] * q[2] - p[2] * q[1], p[2] * q[0] - p[0] * q[2], p[0] * q[1] - p[1] * q[0]]


def rows_of(v, n):
    return [v[i : i + 1] for i in range(n)]


def wide(ref, n):
    return jnp.concatenate([ref[pl.ds(s, n, stride=8), :] for s in range(8)], axis=1)


def narrow(ref, v, first, n):
    for s in range(8):
        ref[pl.ds(8 * first + s, n, stride=8), :] = v[:, s * 128 : (s + 1) * 128]


def metric(x, hs):
    n = x.shape[1]
    u = x[0:1] * x[0:1] + x[1:2] * x[1:2] + x[2:3] * x[2:3] + hs
    one, zero = jnp.ones((1, n), f32), jnp.zeros((3, n), f32)
    lh, lm, ll = split3(jnp.concatenate([-2.0 * x, u, one, zero], 0))
    rh, rm, rl = split3(jnp.concatenate([x, one, u, zero], 0))
    left = jnp.concatenate([lh, lh, lm, lm, lh, ll], 0).astype(bf16)
    right = jnp.concatenate([rh, rm, rh, rm, rl, rh], 0).astype(bf16)
    return left, right


def moments(x, al):
    e = jnp.concatenate([al] + cross(rows_of(x, 3), rows_of(al, 3)) + [jnp.zeros((2, x.shape[1]), f32)], 0)
    f = jnp.concatenate([e, x[0:1] * e, x[1:2] * e, x[2:3] * e], 0)
    return jnp.concatenate(split3(e), 0).astype(bf16), jnp.concatenate(split3(f), 0).astype(bf16)


def finish(x, al, sg, sh):
    xs, a = rows_of(x, 3), rows_of(al, 3)
    g0, g1 = rows_of(sg[0:3], 3), rows_of(sg[3:6], 3)
    sh = -5.0 * sh
    row = lambda p, q: sh[8 * p + q : 8 * p + q + 1]
    h0, h1 = [row(0, q) for q in range(3)], [row(0, 3 + q) for q in range(3)]
    at0 = [a[0] * row(1, q) + a[1] * row(2, q) + a[2] * row(3, q) for q in range(3)]
    at1 = [a[0] * row(1, 3 + q) + a[1] * row(2, 3 + q) + a[2] * row(3, 3 + q) for q in range(3)]
    ax = a[0] * xs[0] + a[1] * xs[1] + a[2] * xs[2]
    c0, c1, c2, c3 = cross(xs, g0), cross(xs, h0), cross(xs, at0), cross(a, g0)
    scale = 1.0 / (4.0 * math.pi)
    vel = [scale * (g1[i] - c0[i]) for i in range(3)]
    stretch = [-scale * (c3[i] + ax * (c1[i] - h1[i]) - c2[i] + at1[i]) for i in range(3)]
    return jnp.concatenate(vel + stretch, 0)


def dot(a, b, dims):
    return lax.dot_general(a, b, (dims, ((), ())), preferred_element_type=f32)


def halves(v):
    h = v.astype(bf16)
    return h, (v - h.astype(f32)).astype(bf16)


def kernels_of(left, right, si, sj):
    y = lax.rsqrt(dot(left, right, ((0,), (0,))))
    y2 = y * y
    p = y2 * y
    t = (si + sj) * y2
    return halves(p + p * t) + halves((p * y2) * (0.6 + t))


def fold(hi, lo, n):
    return (hi[:n] + hi[n : 2 * n] + hi[2 * n :]) + (lo[:n] + lo[n:])


def column(hs):
    return jnp.transpose(jnp.broadcast_to(hs, (128, G)))


def kernel(pos, stg, rad, plist, pcount, vel, stretch,
           own, req, zhb, zlb, reqy, reqn, asend, arecv, bsend, brecv, pa, pb,
           yrecv, hsend, hrecv, nrecv, lsend, lrecv, aop, bop,
           left, right, col, rowj, ea, fa, eb, fb, sga, sha, sgb, shb, sout,
           ssem, rsem):
    y, h, x, l, c = coords()
    bar = pltpu.get_barrier_semaphore()
    peers = (
        [dict(dh=1), dict(dh=3)]
        + [dict(dy=d) for d in (1, 2, 3)]
        + [dict(dl=d) for d in (1, 2, 3)]
        + [dict(dx=dx, dc=dc) for dx, dc in NEAR[1:]]
    )
    for o in peers:
        pl.semaphore_signal(bar, inc=1, device_id=at(**o), device_id_type=MESH)

    used = [0]

    def send(src, dst, **o):
        i = used[0]
        used[0] += 1
        cp = pltpu.make_async_remote_copy(
            src_ref=src, dst_ref=dst, send_sem=ssem.at[i], recv_sem=rsem.at[i],
            device_id=at(**o), device_id_type=MESH)
        cp.start()
        return cp

    sent = []
    narrow(own, pos[...], 0, 3)
    narrow(own, stg[...], 3, 3)
    own[48:56, :] = rad[...]
    k, m, live = plist[0, 0, 0, 1], plist[1, 0, 0, 1], (pcount[0, 0] > 1).astype(jnp.int32)
    ri = lax.broadcasted_iota(jnp.int32, (8, 128), 0)
    req[...] = jnp.where(ri == 0, k, jnp.where(ri == 1, m, live))

    own_x, own_al, own_r = wide(own, 7)[0:3], wide(own, 7)[3:6], wide(own, 7)[6:7]
    own_x = own_x - jnp.mean(own_x, axis=1, keepdims=True)
    own_hs = 0.5 * own_r * own_r
    left[...], right[...] = metric(own_x, own_hs)
    ea[...], fa[...] = moments(own_x, own_al)
    rowj[...] = 1.5 * own_hs
    col[...] = column(1.5 * own_hs)

    def block(i0, j0, two):
        si = jnp.concatenate([col[pl.ds(i0, TI), :]] * (TJ // 128), 1)
        gh, gl, hh, hl = kernels_of(left[:, pl.ds(i0, TI)], right[:, pl.ds(j0, TJ)], si, rowj[:, pl.ds(j0, TJ)])
        d = ((1,), (0,))
        ei, fi = ea[:, pl.ds(i0, TI)], fa[:, pl.ds(i0, TI)]
        sgb[:, pl.ds(j0, TJ)] += fold(dot(ei, gh, d), dot(ei[:16], gl, d), 8)
        shb[:, pl.ds(j0, TJ)] += fold(dot(fi, hh, d), dot(fi[:64], hl, d), 32)
        if two:
            d = ((1,), (1,))
            ej, fj = eb[:, pl.ds(j0, TJ)], fb[:, pl.ds(j0, TJ)]
            sga[:, pl.ds(i0, TI)] += fold(dot(ej, gh, d), dot(ej[:16], gl, d), 8)
            sha[:, pl.ds(i0, TI)] += fold(dot(fj, hh, d), dot(fj[:64], hl, d), 32)

    sgb[...] = jnp.zeros_like(sgb)
    shb[...] = jnp.zeros_like(shb)
    for j0 in range(0, G, TJ):
        block(0, j0, False)

    pl.semaphore_wait(bar, len(peers))

    zh_p = send(own, zhb.at[3], dh=1)
    zh_m = send(own, zhb.at[1], dh=3)
    to_l = [send(own, zlb.at[NL - d], dl=d) for d in (1, 2, 3)]
    to_n = [send(req, reqn.at[((NX - dx) % NX) * NC + dc], dx=dx, dc=dc) for dx, dc in NEAR[1:]]
    to_y = [send(req, reqy.at[NY - d], dy=d) for d in (1, 2, 3)]
    sent += [zh_p, zh_m] + to_l + to_n + to_y
    zhb[0] = own[...]
    zlb[0] = own[...]
    reqn[0] = req[...]
    reqy[0] = req[...]

    for cp in to_l + to_n + to_y:
        cp.wait_recv()

    def want(tile, r):
        return tile[r : r + 1, :]

    def pick(buf, index, n, first):
        out = buf[0]
        for d in range(1, n):
            out = jnp.where(index == (first + d) % n, buf[d], out)
        return out

    near = []
    for i, (dx, dc) in enumerate(NEAR):
        kk = want(reqn[i], 0)
        asend[i] = pick(zlb, (kk // NC) % NL, NL, l)
        if i:
            slot = ((NX - dx) % NX) * NC + dc
            near.append(send(asend.at[i], arecv.at[slot], dx=dx, dc=dc))
    sent += near
    arecv[0] = asend[0]

    zh_p.wait_recv()
    f_p = send(zhb.at[3, pl.ds(0, 24)], zhb.at[2, pl.ds(0, 24)], dh=1)
    zh_m.wait_recv()
    f_m = send(zhb.at[1, pl.ds(24, 32)], zhb.at[2, pl.ds(24, 32)], dh=3)
    sent += [f_p, f_m]

    for j0 in range(0, G, TJ):
        block(TI, j0, False)
    sout[...] = finish(own_x, own_al, sgb[...], shb[...])

    for cp in near:
        cp.wait_recv()
    kk = want(req[...], 0)
    a = arecv[0]
    for i, (dx, dc) in list(enumerate(NEAR))[1:]:
        hit = (kk // (NL * NC) == (x + dx) % NX) & (kk % NC == (c + dc) % NC)
        a = jnp.where(hit, arecv[i], a)
    aop[...] = a
    a7 = wide(aop, 7)
    centre = jnp.mean(a7[0:3], axis=1, keepdims=True)
    ax_, aal, ahs = a7[0:3] - centre, a7[3:6], 0.5 * a7[6:7] * a7[6:7]
    left[...] = metric(ax_, ahs)[0]
    ea[...], fa[...] = moments(ax_, aal)
    col[...] = column(1.5 * ahs)

    f_p.wait_recv()
    f_m.wait_recv()
    along = []
    for d in range(NY):
        mm = want(reqy[d], 1)
        bsend[d] = pick(zhb, mm % NH, NH, h)
        if d:
            along.append(send(bsend.at[d], brecv.at[NY - d], dy=d))
    sent += along
    brecv[0] = bsend[0]
    for cp in along:
        cp.wait_recv()
    mm = want(req[...], 1)
    bop[...] = pick(brecv, mm // NH, NY, y)
    b7 = wide(bop, 7)
    bx_, bal, bhs = b7[0:3] - centre, b7[3:6], 0.5 * b7[6:7] * b7[6:7]
    right[...] = metric(bx_, bhs)[1]
    eb[...], fb[...] = moments(bx_, bal)
    rowj[...] = 1.5 * bhs

    sgb[...] = jnp.zeros_like(sgb)
    shb[...] = jnp.zeros_like(shb)
    sga[...] = jnp.zeros_like(sga)
    sha[...] = jnp.zeros_like(sha)

    def slot1(jj, carry):
        j0 = pl.multiple_of(jj * TJ, TJ)
        for i0 in range(0, G, TI):
            block(i0, j0, True)
        return carry

    lax.fori_loop(0, G // TJ, slot1, 0)
    narrow(pb, finish(bx_, bal, sgb[...], shb[...]), 0, 6)
    back_y = [send(pb, yrecv.at[NY - d], dy=d) for d in (1, 2, 3)]
    yrecv[0] = pb[...]
    narrow(pa, finish(ax_, aal, sga[...], sha[...]), 0, 6)
    back_n = [
        send(pa, nrecv.at[((NX - dx) % NX) * NC + dc], dx=dx, dc=dc) for dx, dc in NEAR[1:]
    ]
    nrecv[0] = pa[...]
    sent += back_y + back_n

    for cp in back_y:
        cp.wait_recv()
    zero = jnp.zeros((48, 128), f32)
    bins = [zero] * NH
    for d in range(NY):
        t = reqy[d]
        kk, mm, on = want(t, 0), want(t, 1), want(t, 2)
        self_pair = (mm == ((y + d) % NY) * NH + h) & (kk == (x * NL + l) * NC + c)
        mine = (on == 1) & (mm // NH == y) & jnp.logical_not(self_pair)
        for e in range(NH):
            bins[e] = bins[e] + jnp.where(mine & (mm % NH == (h + e) % NH), yrecv[d], zero)
    back_h = []
    for e in (2, 1, 3):
        hsend[e] = bins[e]
        back_h.append(send(hsend.at[e], hrecv.at[NH - e], dh=e))
    sent += back_h

    for cp in back_n:
        cp.wait_recv()
    lbins = [zero] * NL
    for i in range(len(NEAR)):
        t = reqn[i]
        kk, on = want(t, 0), want(t, 2)
        mine = (on == 1) & (kk // (NL * NC) == x) & (kk % NC == c)
        for e in range(NL):
            lbins[e] = lbins[e] + jnp.where(mine & ((kk // NC) % NL == (l + e) % NL), nrecv[i], zero)
    back_l = []
    for e in (1, 2, 3):
        lsend[e] = lbins[e]
        back_l.append(send(lsend.at[e], lrecv.at[NL - e], dl=e))
    sent += back_l

    for cp in back_l + back_h:
        cp.wait_recv()
    total = bins[0] + lbins[0]
    for e in (1, 2, 3):
        total = total + lrecv[e] + hrecv[e]
    pa_total = aop
    pa_total[0:48, :] = total
    out = sout[...] + wide(pa_total, 6)
    vel[...] = out[0:3]
    stretch[...] = out[3:6]
    for cp in sent:
        cp.wait_send()
    assert used[0] == N_COPIES


N_COPIES = 2 + 3 + 7 + 3 + 7 + 2 + 3 + 3 + 7 + 3 + 3


def local(positions, strengths, radii, pair_list, pair_count):
    vm, sm = pl.BlockSpec(memory_space=pltpu.VMEM), pl.BlockSpec(memory_space=pltpu.SMEM)
    V = pltpu.VMEM
    out = jax.ShapeDtypeStruct((3, G), f32)
    item, part = (56, 128), (48, 128)
    return pl.pallas_call(
        kernel,
        out_shape=(out, out),
        in_specs=[vm, vm, vm, sm, sm],
        out_specs=(vm, vm),
        scratch_shapes=[
            V(item, f32), V((8, 128), jnp.int32), V((NH,) + item, f32), V((NL,) + item, f32),
            V((NY, 8, 128), jnp.int32), V((8, 8, 128), jnp.int32),
            V((8,) + item, f32), V((8,) + item, f32), V((NY,) + item, f32), V((NY,) + item, f32),
            V(part, f32), V(part, f32),
            V((NY,) + part, f32), V((NH,) + part, f32), V((NH,) + part, f32),
            V((8,) + part, f32), V((NL,) + part, f32), V((NL,) + part, f32),
            V(item, f32), V(item, f32),
            V((48, G), bf16), V((48, G), bf16), V((G, 128), f32), V((1, G), f32),
            V((24, G), bf16), V((96, G), bf16), V((24, G), bf16), V((96, G), bf16),
            V((8, G), f32), V((32, G), f32), V((8, G), f32), V((32, G), f32), V((6, G), f32),
            pltpu.SemaphoreType.DMA((N_COPIES,)), pltpu.SemaphoreType.DMA((N_COPIES,)),
        ],
        compiler_params=pltpu.CompilerParams(
            collective_id=0, has_side_effects=True, vmem_limit_bytes=48 * 2**20
        ),
        cost_estimate=pl.CostEstimate(flops=2 * G * G * 256, bytes_accessed=64 * G, transcendentals=2 * G * G),
        name="vortex_pairs",
    )(positions, strengths, radii.reshape(8, 128), pair_list, pair_count)


def solution(mesh):
    placed = (
        P(None, ("row", "col")),
        P(None, ("row", "col")),
        P(("row", "col")),
        P(None, "row", "col", None),
        P("row", "col"),
    )
    return jax.shard_map(
        local,
        mesh=mesh,
        in_specs=placed,
        out_specs=(P(None, ("row", "col")), P(None, ("row", "col"))),
        check_vma=False,
    )
```

time: 694 us -> 55.5 us (0.08)
  blocking collectives: 294 us -> 0 us
  waiting for transfers between devices: 244 us -> 0 us
  other arithmetic: 118 us -> 0 us
  Pallas kernels: 0 us -> 49.8 us
  between operations: 14 us -> 1.3 us
  local copies, waits for them, and re-layouts: 12.3 us -> 4 us
    all_gather x6 -> x0, blocking collectives: 294 us -> none  [the longest x1 58.6 us: local(): lax.all_gather(strengths, 'col', axis=1, tiled=True)]
    reduce_scatter x2 -> x0, waiting for transfers between devices: 243 us -> none  [the longest x1 145 us: local(): row_part = lax.psum_scatter(row_acc, 'col', scatter_dimension=1, tiled=True)]
    reduce_sum x4 -> x0, other arithmetic: 54.2 us -> none  [the longest x2 30.5 us: pair_terms(): vel_a = -scale * jnp.sum(kern * r_x_b, axis=2)]
    pallas_call x0 -> x1, Pallas kernels: none -> 49.8 us  [local(): pl.pallas_call(kernel, out_shape=(out, out), in_specs=[vm, vm, vm, sm, sm...]
    sub x2 -> x0, other arithmetic: 35.1 us -> none  [cross_rows(): u_a[1] * u_b[2] - u_a[2] * u_b[1]]
    neg x2 -> x0, other arithmetic: 23.4 us -> none  [pair_terms(): str_tb = -scale * jnp.sum(-kern * a_x_b + slope * dot_b * r_x_a, axis=1)]
    dynamic_slice x10 -> x0, local copies, waits for them, and re-layouts: 7.13 us -> none  [the longest x2 2.78 us: visit(): mm = listed[1, slot]]
  transfers between devices with their start and end apart: 2 -> 0, of which waited for: 2 -> 0; matrix products, arithmetic and copies ran while one was open for 0% -> 0% of each run, Pallas kernels for 0% -> 0%
where the time goes in v1:
time: 55.5 us; the launch traced here: 55.2 us
  Pallas kernels  49.8 us (90%)
  local copies, waits for them, and re-layouts  4 us (7%)
  between operations  1.3 us (2%)
    pallas_call x1, Pallas kernels, local(): pl.pallas_call(kernel, out_shape=(out, out), in_specs=[vm, vm, vm, sm, sm...  49.8 us
    unnamed x10, local copies, waits for them, and re-layouts  4 us

profile of v1, /device:TPU:1, one launch (start us, length us, event | category | flops | bytes accessed | tf_op | source)
XLA Modules:
  0.0 55.2 jit_solution(18253027632978773109)
XLA Ops:
  1.3 0.0 copy-start.3
  1.3 0.7 %copy-done.3 = s32[2,1,1,2]{3,2,1,0:T(1,128)S(1)} copy-done((s32[2,1,1,2]{3,2,1,0:T(1,128)S(1)}, s32[2,1,1,2]{3,2,1,0:T(1,128)}, u32[]{:S(2)}) %copy-start.3) | copy-done | bytes 40
  2.0 0.0 copy-start
  2.0 0.7 %copy-done = f32[3,1024]{1,0:T(4,128)S(1)} copy-done((f32[3,1024]{1,0:T(4,128)S(1)}, f32[3,1024]{1,0:T(4,128)}, u32[]{:S(2)}) %copy-start) | copy-done | bytes 12312
  2.7 0.0 copy-start.1
  2.7 0.7 %copy-done.1 = f32[3,1024]{1,0:T(4,128)S(1)} copy-done((f32[3,1024]{1,0:T(4,128)S(1)}, f32[3,1024]{1,0:T(4,128)}, u32[]{:S(2)}) %copy-start.1) | copy-done | bytes 12312
  3.4 0.0 copy-start.2
  3.4 0.7 %copy-done.2 = f32[1024]{0:T(1024)S(1)} copy-done((f32[1024]{0:T(1024)S(1)}, f32[1024]{0:T(1024)}, u32[]{:S(2)}) %copy-start.2) | copy-done | bytes 4120
  4.1 49.8 %vortex_pairs.1 = (f32[3,1024]{1,0:T(4,128)S(1)}, f32[3,1024]{1,0:T(4,128)S(1)}) custom-call(f32[3,1024]{1,0:T(4,128)S(1)} %copy-done, f32[3,1024]{1,0:T(4,128)S(1)} %copy-done.1, f32[8,128]{1,0:T(8,128)S(1)} %bitcast.1, s32[2,1,1,2]{3,2,1,0:T(1,128)S(1)} %copy-done.3, s32[1,1]{1,0:T(1,128)S(6)} %copy.9.pcount), custom_call_target="tpu_custom_call" | custom-call | flops 536870912 | bytes 65536 | tf_op jit(solution)/shard_map/vortex_pairs/pallas_call | solution.py:332
  53.9 0.6 %copy.10 = f32[3,1024]{1,0:T(4,128)} copy(f32[3,1024]{1,0:T(4,128)S(1)} %get-tuple-element.4) | data formatting | bytes 24576
  54.5 0.6 %copy.11 = f32[3,1024]{1,0:T(4,128)} copy(f32[3,1024]{1,0:T(4,128)S(1)} %get-tuple-element.5) | data formatting | bytes 24576
Async XLA Ops:
  1.3 0.7 %copy-start.3 = (s32[2,1,1,2]{3,2,1,0:T(1,128)S(1)}, s32[2,1,1,2]{3,2,1,0:T(1,128)}, u32[]{:S(2)}) copy-start(s32[2,1,1,2]{3,2,1,0:T(1,128)} %plist.1) | copy-start | bytes 52
  2.0 0.7 %copy-start = (f32[3,1024]{1,0:T(4,128)S(1)}, f32[3,1024]{1,0:T(4,128)}, u32[]{:S(2)}) copy-start(f32[3,1024]{1,0:T(4,128)} %pos.1) | copy-start | bytes 36868
  2.7 0.7 %copy-start.1 = (f32[3,1024]{1,0:T(4,128)S(1)}, f32[3,1024]{1,0:T(4,128)}, u32[]{:S(2)}) copy-start(f32[3,1024]{1,0:T(4,128)} %stg.1) | copy-start | bytes 36868
  3.4 0.7 %copy-start.2 = (f32[1024]{0:T(1024)S(1)}, f32[1024]{0:T(1024)}, u32[]{:S(2)}) copy-start(f32[1024]{0:T(1024)} %param.7) | copy-start | bytes 12292

commit v2 on v1

v2 whole, which is shorter than its diff:
```python
import functools
import math

import jax
import jax.numpy as jnp
from jax import lax
from jax.experimental import pallas as pl
from jax.experimental.pallas import tpu as pltpu
from jax.sharding import PartitionSpec as P

G = 1024
MESH = pl.DeviceIdType.MESH
f32, bf16 = jnp.float32, jnp.bfloat16
TJ = 256
NB = G // TJ

NY, NH, NX, NL, NC = 4, 4, 4, 4, 2
NEAR = [(dx, dc) for dx in range(NX) for dc in range(NC)]


def coords():
    r, c = lax.axis_index("row"), lax.axis_index("col")
    return r // NH, r % NH, c // (NL * NC), (c // NC) % NL, c % NC


def at(dy=0, dh=0, dx=0, dl=0, dc=0):
    y, h, x, l, c = coords()
    row = ((y + dy) % NY) * NH + (h + dh) % NH
    col = (((x + dx) % NX) * NL + (l + dl) % NL) * NC + (c + dc) % NC
    return {"row": row, "col": col}


def split3(v):
    h = v.astype(bf16).astype(f32)
    rest = v - h
    m = rest.astype(bf16).astype(f32)
    return h, m, rest - m


def cross(p, q):
    return [p[1] * q[2] - p[2] * q[1], p[2] * q[0] - p[0] * q[2], p[0] * q[1] - p[1] * q[0]]


def rows_of(v, n):
    return [v[i : i + 1] for i in range(n)]


def unpack(ref, half):
    return jnp.concatenate([ref[half, pl.ds(s, 7, stride=4), :] for s in range(4)], axis=1)


def pack(ref, k, v, first, step):
    n = v.shape[0]
    for s in range(step):
        ref[k, pl.ds(step * first + s, n, stride=step), :] = v[:, s * 128 : (s + 1) * 128]


def metric(x, hs):
    n = x.shape[1]
    u = x[0:1] * x[0:1] + x[1:2] * x[1:2] + x[2:3] * x[2:3] + hs
    one, zero = jnp.ones((1, n), f32), jnp.zeros((3, n), f32)
    lh, lm, ll = split3(jnp.concatenate([-2.0 * x, u, one, zero], 0))
    rh, rm, rl = split3(jnp.concatenate([x, one, u, zero], 0))
    left = jnp.concatenate([lh, lh, lm, lm, lh, ll], 0).astype(bf16)
    right = jnp.concatenate([rh, rm, rh, rm, rl, rh], 0).astype(bf16)
    return left, right


def moments(x, al):
    e = jnp.concatenate([al] + cross(rows_of(x, 3), rows_of(al, 3)) + [jnp.zeros((2, x.shape[1]), f32)], 0)
    f = jnp.concatenate([e, x[0:1] * e, x[1:2] * e, x[2:3] * e], 0)
    return jnp.concatenate(split3(e), 0).astype(bf16), jnp.concatenate(split3(f), 0).astype(bf16)


def finish(x, al, sg, sh):
    xs, a = rows_of(x, 3), rows_of(al, 3)
    g0, g1 = rows_of(sg[0:3], 3), rows_of(sg[3:6], 3)
    sh = -5.0 * sh
    row = lambda p, q: sh[8 * p + q : 8 * p + q + 1]
    h0, h1 = [row(0, q) for q in range(3)], [row(0, 3 + q) for q in range(3)]
    at0 = [a[0] * row(1, q) + a[1] * row(2, q) + a[2] * row(3, q) for q in range(3)]
    at1 = [a[0] * row(1, 3 + q) + a[1] * row(2, 3 + q) + a[2] * row(3, 3 + q) for q in range(3)]
    ax = a[0] * xs[0] + a[1] * xs[1] + a[2] * xs[2]
    c0, c1, c2, c3 = cross(xs, g0), cross(xs, h0), cross(xs, at0), cross(a, g0)
    scale = 1.0 / (4.0 * math.pi)
    vel = [scale * (g1[i] - c0[i]) for i in range(3)]
    stretch = [-scale * (c3[i] + ax * (c1[i] - h1[i]) - c2[i] + at1[i]) for i in range(3)]
    return jnp.concatenate(vel + stretch, 0)


def dot(a, b, dims):
    return lax.dot_general(a, b, (dims, ((), ())), preferred_element_type=f32)


def halves(v):
    h = v.astype(bf16)
    return h, (v - h.astype(f32)).astype(bf16)


def kernels_of(left, right, si, sj):
    y = lax.rsqrt(dot(left, right, ((0,), (0,))))
    y2 = y * y
    p = y2 * y
    t = (si + sj) * y2
    return halves(p + p * t) + halves((p * y2) * (0.6 + t))


def fold(hi, lo, n):
    return (hi[:n] + hi[n : 2 * n] + hi[2 * n :]) + (lo[:n] + lo[n:])


def column(hs):
    return jnp.transpose(jnp.broadcast_to(hs, (128, hs.shape[1])))


def kernel(pos_in, stg_in, rad_in, plist, pcount, result,
           pos, stg, rad, own, req, zhb, reqy, reql, nb, lsel, lrecv, bsend, brecv, aop, bop,
           pb, yrecv, hsend, hrecv, pa, lback, nsend, nrecv,
           left, right, col, rowj, ea, fa, eb, fb, sga, sha, sout, lsem, ssem, rsem):
    y, h, x, l, c = coords()
    bar = pltpu.get_barrier_semaphore()
    peers = (
        [dict(dh=1), dict(dh=3)]
        + [dict(dx=dx, dc=dc) for dx, dc in NEAR[1:]]
        + [dict(dl=d) for d in (1, 2, 3)]
        + [dict(dy=d) for d in (1, 2, 3)]
    )
    for o in peers:
        pl.semaphore_signal(bar, inc=1, device_id=at(**o), device_id_type=MESH)
    loads = [
        pltpu.make_async_copy(src, dst, lsem.at[i])
        for i, (src, dst) in enumerate([(pos_in, pos), (stg_in, stg), (rad_in, rad)])
    ]
    for cp in loads:
        cp.start()

    used = [0]
    sent = []

    def send(src, dst, **o):
        i = used[0]
        used[0] += 1
        cp = pltpu.make_async_remote_copy(
            src_ref=src, dst_ref=dst, send_sem=ssem.at[i], recv_sem=rsem.at[i],
            device_id=at(**o), device_id_type=MESH)
        cp.start()
        sent.append(cp)
        return cp

    k, m, live = plist[0, 0, 0, 1], plist[1, 0, 0, 1], (pcount[0, 0] > 1).astype(jnp.int32)
    ri = lax.broadcasted_iota(jnp.int32, (8, 128), 0)
    req[...] = jnp.where(ri == 0, k, jnp.where(ri == 1, m, live))
    for cp in loads:
        cp.wait()
    for half in range(2):
        part = slice(512 * half, 512 * half + 512)
        pack(own, half, pos[:, part], 0, 4)
        pack(own, half, stg[:, part], 3, 4)
        own[half, 24:28, :] = rad[4 * half : 4 * half + 4, :]

    item = jnp.concatenate([unpack(own, 0), unpack(own, 1)], axis=1)
    own_x, own_al, own_r = item[0:3], item[3:6], item[6:7]
    own_x = own_x - jnp.mean(own_x, axis=1, keepdims=True)
    own_hs = 0.5 * own_r * own_r
    left[...], right[...] = metric(own_x, own_hs)
    ea[...], fa[...] = moments(own_x, own_al)
    rowj[...] = 1.5 * own_hs
    col[...] = column(1.5 * own_hs)

    def block(q, two):
        js = pl.ds(q * TJ, TJ)
        si = jnp.concatenate([col[...]] * (TJ // 128), 1)
        gh, gl, hh, hl = kernels_of(left[...], right[:, js], si, rowj[:, js])
        d = ((1,), (0,))
        sg = fold(dot(ea[...], gh, d), dot(ea[:16], gl, d), 8)
        sh = fold(dot(fa[...], hh, d), dot(fa[:64], hl, d), 32)
        if two:
            d = ((1,), (1,))
            ej, fj = eb[:, js], fb[:, js]
            ag = fold(dot(ej, gh, d), dot(ej[:16], gl, d), 8)
            ah = fold(dot(fj, hh, d), dot(fj[:64], hl, d), 32)
            sga[...] = ag if q == 0 else sga[...] + ag
            sha[...] = ah if q == 0 else sha[...] + ah
        return sg, sh

    def own_block(q):
        js = slice(q * TJ, q * TJ + TJ)
        sout[:, js] = finish(own_x[:, js], own_al[:, js], *block(q, False))

    own_block(0)
    own_block(1)
    pl.semaphore_wait(bar, len(peers))

    zh_p = [send(own.at[0], zhb.at[3, 0], dh=1), None]
    zh_m = [None, send(own.at[1], zhb.at[1, 1], dh=3)]
    zh_p[1] = send(own.at[1], zhb.at[3, 1], dh=1)
    zh_m[0] = send(own.at[0], zhb.at[1, 0], dh=3)

    def near_slot(dx, dc):
        return ((NX - dx) % NX) * NC + dc

    near = [send(own, nb.at[near_slot(dx, dc)], dx=dx, dc=dc) for dx, dc in NEAR[1:]]
    ask = [send(req, reql.at[NL - d], dl=d) for d in (1, 2, 3)]
    ask += [send(req, reqy.at[NY - d], dy=d) for d in (1, 2, 3)]
    zhb[0] = own[...]
    nb[0] = own[...]
    reql[0] = req[...]
    reqy[0] = req[...]
    own_block(2)
    own_block(3)

    zh_p[0].wait_recv()
    f_p = send(zhb.at[3, 0], zhb.at[2, 0], dh=1)
    zh_m[1].wait_recv()
    f_m = send(zhb.at[1, 1], zhb.at[2, 1], dh=3)

    def want(tile, r):
        return tile[r : r + 1, :]

    def pick(buf, index, n, first):
        out = buf(0)
        for d in range(1, n):
            out = jnp.where(index == (first + d) % n, buf(d), out)
        return out

    def near_hit(kk, i):
        dx, dc = NEAR[i]
        return (kk // (NL * NC) == (x + dx) % NX) & (kk % NC == (c + dc) % NC)

    for cp in ask + near:
        cp.wait_recv()
    along_l = []
    for d in range(NL):
        kk = want(reql[d], 0)
        a = nb[0]
        for i in range(1, len(NEAR)):
            a = jnp.where(near_hit(kk, i), nb[i], a)
        if d:
            lsel[d] = a
            along_l.append(send(lsel.at[d], lrecv.at[NL - d], dl=d))
        else:
            lrecv[0] = a

    along_y = [[], []]
    for half, cps in enumerate(((zh_m[0], f_p), (zh_p[1], f_m))):
        for cp in cps:
            cp.wait_recv()
        for d in range(NY):
            mm = want(reqy[d], 1)
            b = pick(lambda e: zhb[e, half], mm % NH, NH, h)
            if d:
                bsend[d, half] = b
                along_y[half].append(send(bsend.at[d, half], brecv.at[NY - d, half], dy=d))
            else:
                brecv[0, half] = b

    for cp in along_l:
        cp.wait_recv()
    aop[...] = pick(lambda e: lrecv[e], (want(req[...], 0) // NC) % NL, NL, l)
    item = jnp.concatenate([unpack(aop, 0), unpack(aop, 1)], axis=1)
    centre = jnp.mean(item[0:3], axis=1, keepdims=True)
    ax, aal, ahs = item[0:3] - centre, item[3:6], 0.5 * item[6:7] * item[6:7]
    left[...] = metric(ax, ahs)[0]
    ea[...], fa[...] = moments(ax, aal)
    col[...] = column(1.5 * ahs)

    def column_half(half):
        for cp in along_y[half]:
            cp.wait_recv()
        bop[half] = pick(lambda e: brecv[e, half], want(req[...], 1) // NH, NY, y)
        item = unpack(bop, half)
        bx, bal, bhs = item[0:3] - centre, item[3:6], 0.5 * item[6:7] * item[6:7]
        js = pl.ds(512 * half, 512)
        right[:, js] = metric(bx, bhs)[1]
        eb[:, js], fb[:, js] = moments(bx, bal)
        rowj[:, js] = 1.5 * bhs
        return bx, bal

    back_y, sums = [None] * NB, [None] * NB

    def give_back(q):
        bx, bal = cols[q // 2]
        js = slice((q % 2) * TJ, (q % 2) * TJ + TJ)
        pack(pb, q, finish(bx[:, js], bal[:, js], *sums[q]), 0, 2)
        back_y[q] = [send(pb.at[q], yrecv.at[NY - d, q], dy=d) for d in (1, 2, 3)]
        yrecv[0, q] = pb[q]

    cols = [column_half(0)]
    sums[0] = block(0, True)
    sums[1] = block(1, True)
    cols.append(column_half(1))
    give_back(0)
    sums[2] = block(2, True)
    give_back(1)
    sums[3] = block(3, True)
    give_back(2)
    give_back(3)
    back_l = []
    rows = finish(ax, aal, sga[...], sha[...])
    for half in range(2):
        pack(pa, half, rows[:, 512 * half : 512 * half + 512], 0, 4)
        back_l.append([send(pa.at[half], lback.at[NL - d, half], dl=d) for d in (1, 2, 3)])
        lback[0, half] = pa[half]

    masks = []
    for d in range(NY):
        t = reqy[d]
        kk, mm, on = want(t, 0), want(t, 1), want(t, 2)
        self_pair = (mm == ((y + d) % NY) * NH + h) & (kk == (x * NL + l) * NC + c)
        mine = (on == 1) & (mm // NH == y) & jnp.logical_not(self_pair)
        masks.append([mine & (mm % NH == (h + e) % NH) for e in range(NH)])
    back_h = []
    for q in range(NB):
        for cp in back_y[q]:
            cp.wait_recv()
        for e in (2, 1, 3, 0):
            total = jnp.zeros((12, 128), f32)
            for d in range(NY):
                total = total + jnp.where(masks[d][e], yrecv[d, q], 0.0)
            if e:
                hsend[e, q] = total
                back_h.append(send(hsend.at[e, q], hrecv.at[NH - e, q], dh=e))
            else:
                hrecv[0, q] = total

    masks = []
    for d in range(NL):
        t = reql[d]
        kk, on = want(t, 0), want(t, 2)
        mine = (on == 1) & ((kk // NC) % NL == l)
        masks.append([mine & near_hit(kk, i) for i in range(len(NEAR))])
    back_n = []
    for half in range(2):
        for cp in back_l[half]:
            cp.wait_recv()
        for i in list(range(1, len(NEAR))) + [0]:
            total = jnp.zeros((24, 128), f32)
            for d in range(NL):
                total = total + jnp.where(masks[d][i], lback[d, half], 0.0)
            if i:
                nsend[i, half] = total
                dx, dc = NEAR[i]
                back_n.append(send(nsend.at[i, half], nrecv.at[near_slot(dx, dc), half], dx=dx, dc=dc))
            else:
                nrecv[0, half] = total

    for cp in sent:
        cp.wait_send()
    for cp in back_n:
        cp.wait_recv()
    for half in range(2):
        total = nrecv[0, half]
        for i in range(1, len(NEAR)):
            total = total + nrecv[i, half]
        pa[half] = total
    for cp in back_h:
        cp.wait_recv()
    for q in range(NB):
        pb[q] = (hrecv[0, q] + hrecv[1, q]) + (hrecv[2, q] + hrecv[3, q])
    for t in range(8):
        lanes = slice(128 * t, 128 * t + 128)
        out = (sout[:, lanes] + pa[t // 4, pl.ds(t % 4, 6, stride=4), :]
               + pb[t // 2, pl.ds(t % 2, 6, stride=2), :])
        result[:, lanes] = out
    assert used[0] == N_COPIES


N_COPIES = 4 + 7 + 6 + 2 + 3 + 6 + 12 + 6 + 12 + 14


def local(positions, strengths, radii, pair_list, pair_count):
    vm, sm = pl.BlockSpec(memory_space=pltpu.VMEM), pl.BlockSpec(memory_space=pltpu.SMEM)
    hbm = pl.BlockSpec(memory_space=pltpu.HBM)
    V = pltpu.VMEM
    out = jax.ShapeDtypeStruct((6, G), f32)
    item = (2, 28, 128)
    result = pl.pallas_call(
        kernel,
        out_shape=out,
        in_specs=[hbm, hbm, hbm, sm, sm],
        out_specs=vm,
        scratch_shapes=[
            V((3, G), f32), V((3, G), f32), V((8, 128), f32),
            V(item, f32), V((8, 128), jnp.int32), V((NH,) + item, f32),
            V((NY, 8, 128), jnp.int32), V((NL, 8, 128), jnp.int32),
            V((8,) + item, f32), V((NL,) + item, f32), V((NL,) + item, f32),
            V((NY,) + item, f32), V((NY,) + item, f32), V(item, f32), V(item, f32),
            V((NB, 12, 128), f32), V((NY, NB, 12, 128), f32), V((NH, NB, 12, 128), f32), V((NH, NB, 12, 128), f32),
            V((2, 24, 128), f32), V((NL, 2, 24, 128), f32), V((8, 2, 24, 128), f32), V((8, 2, 24, 128), f32),
            V((48, G), bf16), V((48, G), bf16), V((G, 128), f32), V((1, G), f32),
            V((24, G), bf16), V((96, G), bf16), V((24, G), bf16), V((96, G), bf16),
            V((8, G), f32), V((32, G), f32), V((6, G), f32),
            pltpu.SemaphoreType.DMA((3,)), pltpu.SemaphoreType.DMA((N_COPIES,)), pltpu.SemaphoreType.DMA((N_COPIES,)),
        ],
        compiler_params=pltpu.CompilerParams(
            collective_id=0, has_side_effects=True, vmem_limit_bytes=64 * 2**20 - 2**16
        ),
        cost_estimate=pl.CostEstimate(flops=2 * G * G * 256, bytes_accessed=64 * G, transcendentals=2 * G * G),
        name="vortex_pairs",
    )(positions, strengths, radii.reshape(8, 128), pair_list, pair_count)
    return result[:3], result[3:]


def solution(mesh):
    placed = (
        P(None, ("row", "col")),
        P(None, ("row", "col")),
        P(("row", "col")),
        P(None, "row", "col", None),
        P("row", "col"),
    )
    return jax.shard_map(
        local,
        mesh=mesh,
        in_specs=placed,
        out_specs=(P(None, ("row", "col")), P(None, ("row", "col"))),
        check_vma=False,
    )
```

time: 55.5 us -> 49.8 us (0.90)
  Pallas kernels: 49.8 us -> 46.8 us
  local copies, waits for them, and re-layouts: 4 us -> 1.45 us
    unnamed x10 -> x0, local copies, waits for them, and re-layouts: 4 us -> none
    pallas_call x1, Pallas kernels: 49.8 us -> 46.8 us  [local(): pl.pallas_call(kernel, out_shape=out, in_specs=[hbm, hbm, hbm, sm, sm], o...]
    slice x0 -> x1, local copies, waits for them, and re-layouts: none -> 1.45 us  [local(): return (result[:3], result[3:])]
where the time goes in v2:
time: 49.8 us; the launch traced here: 49.6 us
  Pallas kernels  46.8 us (94%)
  local copies, waits for them, and re-layouts  1.45 us (3%)
  between operations  1.29 us (3%)
    pallas_call x1, Pallas kernels, local(): pl.pallas_call(kernel, out_shape=out, in_specs=[hbm, hbm, hbm, sm, sm], o...  46.8 us
    slice x1, local copies, waits for them, and re-layouts, local(): return (result[:3], result[3:])  1.45 us

profile of v2, /device:TPU:1, one launch (start us, length us, event | category | flops | bytes accessed | tf_op | source)
XLA Modules:
  0.0 49.6 jit_solution(1934330908392337710)
XLA Ops:
  1.3 46.8 %vortex_pairs.1 = f32[6,1024]{1,0:T(8,128)} custom-call(f32[3,1024]{1,0:T(4,128)} %pos_in.1, f32[3,1024]{1,0:T(4,128)} %stg_in.1, f32[8,128]{1,0:T(8,128)} %bitcast.1, s32[2,1,1,2]{3,2,1,0:T(1,128)} %plist.1, s32[1,1]{1,0:T(1,128)S(6)} %copy.7.pcount), custom_call_target="tpu_custom_call" | custom-call | flops 536870912 | bytes 65536 | tf_op jit(solution)/shard_map/vortex_pairs/pallas_call | solution.py:377
  48.1 1.5 %fusion = (f32[3,1024]{1,0:T(4,128)}, f32[3,1024]{1,0:T(4,128)}) fusion(f32[6,1024]{1,0:T(8,128)} %vortex_pairs.1), kind=kLoop, calls=%fused_computation | loop fusion | bytes 49152 | tf_op jit(solution)/shard_map/slice | solution.py:401

commit v3 on v2

v3 whole, which is shorter than its diff:
```python
import functools
import math

import jax
import jax.numpy as jnp
from jax import lax
from jax.experimental import pallas as pl
from jax.experimental.pallas import tpu as pltpu
from jax.sharding import PartitionSpec as P

G = 1024
MESH = pl.DeviceIdType.MESH
f32, bf16 = jnp.float32, jnp.bfloat16
TJ = 256
NB = G // TJ

NY, NH, NX, NL, NC = 4, 4, 4, 4, 2
NEAR = [(dx, dc) for dx in range(NX) for dc in range(NC)]


def coords():
    r, c = lax.axis_index("row"), lax.axis_index("col")
    return r // NH, r % NH, c // (NL * NC), (c // NC) % NL, c % NC


def at(dy=0, dh=0, dx=0, dl=0, dc=0):
    y, h, x, l, c = coords()
    row = ((y + dy) % NY) * NH + (h + dh) % NH
    col = (((x + dx) % NX) * NL + (l + dl) % NL) * NC + (c + dc) % NC
    return {"row": row, "col": col}


def split3(v):
    h = v.astype(bf16).astype(f32)
    rest = v - h
    m = rest.astype(bf16).astype(f32)
    return h, m, rest - m


def cross(p, q):
    return [p[1] * q[2] - p[2] * q[1], p[2] * q[0] - p[0] * q[2], p[0] * q[1] - p[1] * q[0]]


def rows_of(v, n):
    return [v[i : i + 1] for i in range(n)]


def unpack(ref, q):
    return jnp.concatenate([ref[q, pl.ds(s, 7, stride=2), :] for s in range(2)], axis=1)


def unpack_all(ref):
    return jnp.concatenate([unpack(ref, q) for q in range(NB)], axis=1)


def pack(ref, q, v, first):
    for s in range(2):
        ref[q, pl.ds(2 * first + s, v.shape[0], stride=2), :] = v[:, s * 128 : (s + 1) * 128]


def metric(x, hs):
    n = x.shape[1]
    u = x[0:1] * x[0:1] + x[1:2] * x[1:2] + x[2:3] * x[2:3] + hs
    one, zero = jnp.ones((1, n), f32), jnp.zeros((3, n), f32)
    lh, lm, ll = split3(jnp.concatenate([-2.0 * x, u, one, zero], 0))
    rh, rm, rl = split3(jnp.concatenate([x, one, u, zero], 0))
    left = jnp.concatenate([lh, lh, lm, lm, lh, ll], 0).astype(bf16)
    right = jnp.concatenate([rh, rm, rh, rm, rl, rh], 0).astype(bf16)
    return left, right


def moments(x, al):
    e = jnp.concatenate([al] + cross(rows_of(x, 3), rows_of(al, 3)) + [jnp.zeros((2, x.shape[1]), f32)], 0)
    f = jnp.concatenate([e, x[0:1] * e, x[1:2] * e, x[2:3] * e], 0)
    return jnp.concatenate(split3(e), 0).astype(bf16), jnp.concatenate(split3(f), 0).astype(bf16)


def finish(x, al, sg, sh):
    xs, a = rows_of(x, 3), rows_of(al, 3)
    g0, g1 = rows_of(sg[0:3], 3), rows_of(sg[3:6], 3)
    sh = -5.0 * sh
    row = lambda p, q: sh[8 * p + q : 8 * p + q + 1]
    h0, h1 = [row(0, q) for q in range(3)], [row(0, 3 + q) for q in range(3)]
    at0 = [a[0] * row(1, q) + a[1] * row(2, q) + a[2] * row(3, q) for q in range(3)]
    at1 = [a[0] * row(1, 3 + q) + a[1] * row(2, 3 + q) + a[2] * row(3, 3 + q) for q in range(3)]
    ax = a[0] * xs[0] + a[1] * xs[1] + a[2] * xs[2]
    c0, c1, c2, c3 = cross(xs, g0), cross(xs, h0), cross(xs, at0), cross(a, g0)
    scale = 1.0 / (4.0 * math.pi)
    vel = [scale * (g1[i] - c0[i]) for i in range(3)]
    stretch = [-scale * (c3[i] + ax * (c1[i] - h1[i]) - c2[i] + at1[i]) for i in range(3)]
    return jnp.concatenate(vel + stretch, 0)


def dot(a, b, dims):
    return lax.dot_general(a, b, (dims, ((), ())), preferred_element_type=f32)


def halves(v):
    h = v.astype(bf16)
    return h, (v - h.astype(f32)).astype(bf16)


def kernels_of(left, right, si, sj):
    y = lax.rsqrt(dot(left, right, ((0,), (0,))))
    y2 = y * y
    p = y2 * y
    t = (si + sj) * y2
    return halves(p + p * t) + halves((p * y2) * (0.6 + t))


def fold(hi, lo, n):
    return (hi[:n] + hi[n : 2 * n] + hi[2 * n :]) + (lo[:n] + lo[n:])


def column(hs):
    return jnp.transpose(jnp.broadcast_to(hs, (128, hs.shape[1])))


def kernel(pos_in, stg_in, rad_in, plist, pcount, result,
           pos, stg, rad, own, req, zhb, reqy, reql, reqn, nb, lsel, lrecv, bsend, brecv, aop, bop,
           pb, yrecv, hsend, hrecv, pa, nrecv, lsend, lback,
           left, right, col, rowj, ea, fa, eb, fb, kept, sout, lsem, ssem, rsem):
    y, h, x, l, c = coords()
    bar = pltpu.get_barrier_semaphore()
    peers = (
        [dict(dh=1), dict(dh=3)]
        + [dict(dx=dx, dc=dc) for dx, dc in NEAR[1:]]
        + [dict(dl=d) for d in (1, 2, 3)]
        + [dict(dy=d) for d in (1, 2, 3)]
    )
    @pl.when(h == 0)
    def _():
        pl.semaphore_signal(bar, inc=1, device_id=at(dh=2), device_id_type=MESH)

    for o in peers:
        pl.semaphore_signal(bar, inc=1, device_id=at(**o), device_id_type=MESH)
    loads = [
        pltpu.make_async_copy(src, dst, lsem.at[i])
        for i, (src, dst) in enumerate([(pos_in, pos), (stg_in, stg), (rad_in, rad)])
    ]
    for cp in loads:
        cp.start()

    used = [0]
    sent = []

    def slot():
        used[0] += 1
        return used[0] - 1

    def prep(src, dst, i, r, **o):
        return pltpu.make_async_remote_copy(
            src_ref=src, dst_ref=dst, send_sem=ssem.at[i], recv_sem=rsem.at[r],
            device_id=at(**o), device_id_type=MESH)

    def send(src, dst, **o):
        i = slot()
        cp = prep(src, dst, i, i, **o)
        cp.start()
        sent.append(cp)
        return cp

    k, m, live = plist[0, 0, 0, 1], plist[1, 0, 0, 1], (pcount[0, 0] > 1).astype(jnp.int32)
    ri = lax.broadcasted_iota(jnp.int32, (8, 128), 0)
    req[...] = jnp.where(ri == 0, k, jnp.where(ri == 1, m, live))
    for cp in loads:
        cp.wait()
    for q in range(NB):
        js = slice(TJ * q, TJ * q + TJ)
        pack(own, q, pos[:, js], 0)
        pack(own, q, stg[:, js], 3)
        own[q, 12:14, :] = rad[2 * q : 2 * q + 2, :]

    item = unpack_all(own)
    own_x, own_al, own_r = item[0:3], item[3:6], item[6:7]
    own_x = own_x - jnp.mean(own_x, axis=1, keepdims=True)
    own_hs = 0.5 * own_r * own_r
    left[...], right[...] = metric(own_x, own_hs)
    ea[...], fa[...] = moments(own_x, own_al)
    rowj[...] = 1.5 * own_hs
    col[...] = column(1.5 * own_hs)

    def block(q, keep):
        js = pl.ds(q * TJ, TJ)
        si = jnp.concatenate([col[...]] * (TJ // 128), 1)
        parts = kernels_of(left[...], right[:, js], si, rowj[:, js])
        gh, gl, hh, hl = parts
        if keep:
            for i in range(4):
                kept[i, :, js] = parts[i]
        d = ((1,), (0,))
        sg = fold(dot(ea[...], gh, d), dot(ea[:16], gl, d), 8)
        sh = fold(dot(fa[...], hh, d), dot(fa[:64], hl, d), 32)
        return sg, sh

    def row_block(p):
        rs = pl.ds(p * TJ, TJ)
        d = ((1,), (1,))
        sg = fold(dot(eb[...], kept[0, rs, :], d), dot(eb[:16], kept[1, rs, :], d), 8)
        sh = fold(dot(fb[...], kept[2, rs, :], d), dot(fb[:64], kept[3, rs, :], d), 32)
        return sg, sh

    def own_block(q):
        js = slice(q * TJ, q * TJ + TJ)
        sout[:, js] = finish(own_x[:, js], own_al[:, js], *block(q, False))

    pl.semaphore_wait(bar, len(peers) + (h // 2) * (1 - h % 2))
    ways = ((1, 0), (3, 2), (1, 1), (3, 3))
    ahead, across = {}, {}
    for d, q in ways:
        i = slot()
        ahead[q] = prep(zhb.at[NH - d, pl.ds(q, 1)], zhb.at[2, pl.ds(q, 1)], i, i, dh=d)
        across[q] = prep(own.at[pl.ds(q, 1)], zhb.at[2, pl.ds(q, 1)], slot(), i, dh=2)

    @pl.when(h == 2)
    def _():
        for d, q in ways:
            across[q].start()

    def to_zh(q, n, d):
        return send(own.at[pl.ds(q, n)], zhb.at[NH - d, pl.ds(q, n)], dh=d)

    first = {(d, q): to_zh(q, 1, d) for d, q in ways}
    rest = {1: to_zh(2, 2, 1), 3: to_zh(0, 2, 3)}

    def near_slot(dx, dc):
        return ((NX - dx) % NX) * NC + dc

    ask_y = [send(req, reqy.at[NY - d], dy=d) for d in (1, 2, 3)]
    ask_l = [send(req, reql.at[NL - d], dl=d) for d in (1, 2, 3)]
    near = [
        [send(own.at[pl.ds(q, 2)], nb.at[near_slot(dx, dc), pl.ds(q, 2)], dx=dx, dc=dc) for dx, dc in NEAR[1:]]
        for q in (0, 2)
    ]
    ask_n = [send(req, reqn.at[near_slot(dx, dc)], dx=dx, dc=dc) for dx, dc in NEAR[1:]]
    zhb[0] = own[...]
    nb[0] = own[...]
    reql[0] = req[...]
    reqy[0] = req[...]
    reqn[0] = req[...]
    for q in range(NB):
        own_block(q)

    for d, q in ways:
        first[d, q].wait_recv()

        @pl.when(h != NH - d)
        def _():
            ahead[q].start()

    def want(tile, r):
        return tile[r : r + 1, :]

    def pick(buf, index, n, first):
        out = buf(0)
        for d in range(1, n):
            out = jnp.where(index == (first + d) % n, buf(d), out)
        return out

    def near_hit(kk, i):
        dx, dc = NEAR[i]
        return (kk // (NL * NC) == (x + dx) % NX) & (kk % NC == (c + dc) % NC)

    for cp in ask_l:
        cp.wait_recv()
    along_l = []
    for half in range(2):
        for cp in near[half]:
            cp.wait_recv()
        qs = pl.ds(2 * half, 2)
        for d in (1, 2, 3, 0):
            kk = want(reql[d], 0)
            a = nb[0, qs]
            for i in range(1, len(NEAR)):
                a = jnp.where(near_hit(kk, i), nb[i, qs], a)
            if d:
                lsel[d, qs] = a
                along_l.append(send(lsel.at[d, qs], lrecv.at[NL - d, qs], dl=d))
            else:
                lrecv[0, qs] = a

    for cp in ask_y + list(rest.values()):
        cp.wait_recv()
    order = (0, 2, 1, 3)
    along_y = {}
    for q in order:
        ahead[q].wait_recv()
        along_y[q] = []
        for d in (2, 1, 3, 0):
            b = pick(lambda e: zhb[e, q], want(reqy[d], 1) % NH, NH, h)
            if d:
                bsend[d, q] = b
                along_y[q].append(send(bsend.at[d, q], brecv.at[NY - d, q], dy=d))
            else:
                brecv[0, q] = b

    for cp in along_l:
        cp.wait_recv()
    aop[...] = pick(lambda e: lrecv[e], (want(req[...], 0) // NC) % NL, NL, l)
    item = unpack_all(aop)
    centre = jnp.mean(item[0:3], axis=1, keepdims=True)
    ax, aal, ahs = item[0:3] - centre, item[3:6], 0.5 * item[6:7] * item[6:7]
    left[...] = metric(ax, ahs)[0]
    ea[...], fa[...] = moments(ax, aal)
    col[...] = column(1.5 * ahs)

    back_y = {}
    for q in order:
        for cp in along_y[q]:
            cp.wait_recv()
        bop[q] = pick(lambda e: brecv[e, q], want(req[...], 1) // NH, NY, y)
        item = unpack(bop, q)
        bx, bal, bhs = item[0:3] - centre, item[3:6], 0.5 * item[6:7] * item[6:7]
        js = pl.ds(q * TJ, TJ)
        right[:, js] = metric(bx, bhs)[1]
        eb[:, js], fb[:, js] = moments(bx, bal)
        rowj[:, js] = 1.5 * bhs
        pack(pb, q, finish(bx, bal, *block(q, True)), 0)
        back_y[q] = [send(pb.at[q], yrecv.at[NY - d, q], dy=d) for d in (2, 1, 3)]
        yrecv[0, q] = pb[q]

    masks_h = []
    for d in range(NY):
        t = reqy[d]
        kk, mm, on = want(t, 0), want(t, 1), want(t, 2)
        self_pair = (mm == ((y + d) % NY) * NH + h) & (kk == (x * NL + l) * NC + c)
        mine = (on == 1) & (mm // NH == y) & jnp.logical_not(self_pair)
        masks_h.append([mine & (mm % NH == (h + e) % NH) for e in range(NH)])
    back_h = []

    def to_owner_h(q, es):
        for e in es:
            total = jnp.zeros((12, 128), f32)
            for d in range(NY):
                total = total + jnp.where(masks_h[d][e], yrecv[d, q], 0.0)
            if e:
                hsend[e, q] = total
                back_h.append(send(hsend.at[e, q], hrecv.at[NH - e, q], dh=e))
            else:
                hrecv[0, q] = total

    back_n = []
    for p, q in enumerate(order):
        rs = slice(p * TJ, p * TJ + TJ)
        pack(pa, p, finish(ax[:, rs], aal[:, rs], *row_block(p)), 0)
        back_n.append([send(pa.at[p], nrecv.at[near_slot(dx, dc), p], dx=dx, dc=dc) for dx, dc in NEAR[1:]])
        nrecv[0, p] = pa[p]
        for cp in back_y[q]:
            cp.wait_recv()
        to_owner_h(q, (2,))
        if p:
            to_owner_h(order[p - 1], (1, 3))
    to_owner_h(order[3], (1, 3))

    for cp in ask_n:
        cp.wait_recv()
    masks_l = []
    for i in range(len(NEAR)):
        t = reqn[i]
        kk, on = want(t, 0), want(t, 2)
        mine = (on == 1) & (kk // (NL * NC) == x) & (kk % NC == c)
        masks_l.append([mine & ((kk // NC) % NL == (l + e) % NL) for e in range(NL)])
    back_l = []
    for p in range(NB):
        for cp in back_n[p]:
            cp.wait_recv()
        for e in (3, 2, 1, 0):
            total = jnp.zeros((12, 128), f32)
            for i in range(len(NEAR)):
                total = total + jnp.where(masks_l[i][e], nrecv[i, p], 0.0)
            if e:
                lsend[e, p] = total
                back_l.append(send(lsend.at[e, p], lback.at[NL - e, p], dl=e))
            else:
                lback[0, p] = total

    for q in range(NB):
        to_owner_h(q, (0,))
    for cp in sent:
        cp.wait_send()

    @pl.when(h == 2)
    def _():
        for cp in across.values():
            cp.wait_send()

    for d in (1, 3):
        @pl.when(h != NH - d)
        def _():
            for e, q in ways:
                if e == d:
                    ahead[q].wait_send()

    for cp in back_l + back_h:
        cp.wait_recv()
    for q in range(NB):
        pb[q] = ((hrecv[0, q] + hrecv[1, q]) + (hrecv[2, q] + hrecv[3, q])) + (
            (lback[0, q] + lback[1, q]) + (lback[2, q] + lback[3, q]))
    for t in range(8):
        lanes = slice(128 * t, 128 * t + 128)
        result[:, lanes] = sout[:, lanes] + pb[t // 2, pl.ds(t % 2, 6, stride=2), :]
    assert used[0] == N_COPIES


N_COPIES = 6 + 3 + 3 + 14 + 7 + 8 + 6 + 12 + 12 + 28 + 12 + 12


def local(positions, strengths, radii, pair_list, pair_count):
    vm, sm = pl.BlockSpec(memory_space=pltpu.VMEM), pl.BlockSpec(memory_space=pltpu.SMEM)
    hbm = pl.BlockSpec(memory_space=pltpu.HBM)
    V = pltpu.VMEM
    out = jax.ShapeDtypeStruct((6, G), f32)
    item, part = (NB, 14, 128), (NB, 12, 128)
    ask = (8, 128)
    result = pl.pallas_call(
        kernel,
        out_shape=out,
        in_specs=[hbm, hbm, hbm, sm, sm],
        out_specs=vm,
        scratch_shapes=[
            V((3, G), f32), V((3, G), f32), V((8, 128), f32),
            V(item, f32), V(ask, jnp.int32), V((NH,) + item, f32),
            V((NY,) + ask, jnp.int32), V((NL,) + ask, jnp.int32), V((8,) + ask, jnp.int32),
            V((8,) + item, f32), V((NL,) + item, f32), V((NL,) + item, f32),
            V((NY,) + item, f32), V((NY,) + item, f32), V(item, f32), V(item, f32),
            V(part, f32), V((NY,) + part, f32), V((NH,) + part, f32), V((NH,) + part, f32),
            V(part, f32), V((8,) + part, f32), V((NL,) + part, f32), V((NL,) + part, f32),
            V((48, G), bf16), V((48, G), bf16), V((G, 128), f32), V((1, G), f32),
            V((24, G), bf16), V((96, G), bf16), V((24, G), bf16), V((96, G), bf16),
            V((4, G, G), bf16), V((6, G), f32),
            pltpu.SemaphoreType.DMA((3,)), pltpu.SemaphoreType.DMA((N_COPIES,)), pltpu.SemaphoreType.DMA((N_COPIES,)),
        ],
        compiler_params=pltpu.CompilerParams(
            collective_id=0, has_side_effects=True, vmem_limit_bytes=64 * 2**20 - 2**16
        ),
        cost_estimate=pl.CostEstimate(flops=2 * G * G * 256, bytes_accessed=64 * G, transcendentals=2 * G * G),
        name="vortex_pairs",
    )(positions, strengths, radii.reshape(8, 128), pair_list, pair_count)
    return result[:3], result[3:]


def solution(mesh):
    placed = (
        P(None, ("row", "col")),
        P(None, ("row", "col")),
        P(("row", "col")),
        P(None, "row", "col", None),
        P("row", "col"),
    )
    return jax.shard_map(
        local,
        mesh=mesh,
        in_specs=placed,
        out_specs=(P(None, ("row", "col")), P(None, ("row", "col"))),
        check_vma=False,
    )
```

time: 49.8 us -> 47.8 us (0.960)
  Pallas kernels: 46.8 us -> 44.8 us
    pallas_call x1, Pallas kernels: 46.8 us -> 44.8 us  [local(): pl.pallas_call(kernel, out_shape=out, in_specs=[hbm, hbm, hbm, sm, sm], o...]
where the time goes in v3:
time: 47.8 us; the launch traced here: 47.5 us
  Pallas kernels  44.8 us (94%)
  local copies, waits for them, and re-layouts  1.45 us (3%)
  between operations  1.29 us (3%)
    pallas_call x1, Pallas kernels, local(): pl.pallas_call(kernel, out_shape=out, in_specs=[hbm, hbm, hbm, sm, sm], o...  44.8 us
    slice x1, local copies, waits for them, and re-layouts, local(): return (result[:3], result[3:])  1.45 us

profile of v3, /device:TPU:1, one launch (start us, length us, event | category | flops | bytes accessed | tf_op | source)
XLA Modules:
  0.0 47.5 jit_solution(8644935414412013395)
XLA Ops:
  1.3 44.8 %vortex_pairs.1 = f32[6,1024]{1,0:T(8,128)} custom-call(f32[3,1024]{1,0:T(4,128)} %pos_in.1, f32[3,1024]{1,0:T(4,128)} %stg_in.1, f32[8,128]{1,0:T(8,128)} %bitcast.1, s32[2,1,1,2]{3,2,1,0:T(1,128)} %plist.1, s32[1,1]{1,0:T(1,128)S(6)} %copy.7.pcount), custom_call_target="tpu_custom_call" | custom-call | flops 536870912 | bytes 65536 | tf_op jit(solution)/shard_map/vortex_pairs/pallas_call | solution.py:415
  46.1 1.5 %fusion = (f32[3,1024]{1,0:T(4,128)}, f32[3,1024]{1,0:T(4,128)}) fusion(f32[6,1024]{1,0:T(8,128)} %vortex_pairs.1), kind=kLoop, calls=%fused_computation | loop fusion | bytes 49152 | tf_op jit(solution)/shard_map/slice | solution.py:439

commit v4 on v3

--- a/solution.py
+++ b/solution.py
@@ -53,9 +53,9 @@
     return jnp.concatenate([unpack(ref, q) for q in range(NB)], axis=1)
 
 
-def pack(ref, q, v, first):
+def pack(ref, q, v):
     for s in range(2):
-        ref[q, pl.ds(2 * first + s, v.shape[0], stride=2), :] = v[:, s * 128 : (s + 1) * 128]
+        ref[q, pl.ds(s, 6, stride=2), :] = v[:, s * 128 : (s + 1) * 128]
 
 
 def metric(x, hs):
@@ -167,8 +167,7 @@
         cp.wait()
     for q in range(NB):
         js = slice(TJ * q, TJ * q + TJ)
-        pack(own, q, pos[:, js], 0)
-        pack(own, q, stg[:, js], 3)
+        pack(own, q, jnp.concatenate([pos[:, js], stg[:, js]], axis=0))
         own[q, 12:14, :] = rad[2 * q : 2 * q + 2, :]
 
     item = unpack_all(own)
@@ -315,7 +314,7 @@
         right[:, js] = metric(bx, bhs)[1]
         eb[:, js], fb[:, js] = moments(bx, bal)
         rowj[:, js] = 1.5 * bhs
-        pack(pb, q, finish(bx, bal, *block(q, True)), 0)
+        pack(pb, q, finish(bx, bal, *block(q, True)))
         back_y[q] = [send(pb.at[q], yrecv.at[NY - d, q], dy=d) for d in (2, 1, 3)]
         yrecv[0, q] = pb[q]
 
@@ -342,7 +341,7 @@
     back_n = []
     for p, q in enumerate(order):
         rs = slice(p * TJ, p * TJ + TJ)
-        pack(pa, p, finish(ax[:, rs], aal[:, rs], *row_block(p)), 0)
+        pack(pa, p, finish(ax[:, rs], aal[:, rs], *row_block(p)))
         back_n.append([send(pa.at[p], nrecv.at[near_slot(dx, dc), p], dx=dx, dc=dc) for dx, dc in NEAR[1:]])
         nrecv[0, p] = pa[p]
         for cp in back_y[q]:

time: 47.8 us -> 47.8 us (level)
  no operation moved by 1% of the time
where the time goes in v4:
time: 47.8 us; the launch traced here: 47.5 us
  Pallas kernels  44.8 us (94%)
  local copies, waits for them, and re-layouts  1.45 us (3%)
  between operations  1.29 us (3%)
    pallas_call x1, Pallas kernels, local(): pl.pallas_call(kernel, out_shape=out, in_specs=[hbm, hbm, hbm, sm, sm], o...  44.8 us
    slice x1, local copies, waits for them, and re-layouts, local(): return (result[:3], result[3:])  1.45 us

profile of v4, /device:TPU:1, one launch (start us, length us, event | category | flops | bytes accessed | tf_op | source)
XLA Modules:
  0.0 47.5 jit_solution(15663349013084663804)
XLA Ops:
  1.3 44.8 %vortex_pairs.1 = f32[6,1024]{1,0:T(8,128)} custom-call(f32[3,1024]{1,0:T(4,128)} %pos_in.1, f32[3,1024]{1,0:T(4,128)} %stg_in.1, f32[8,128]{1,0:T(8,128)} %bitcast.1, s32[2,1,1,2]{3,2,1,0:T(1,128)} %plist.1, s32[1,1]{1,0:T(1,128)S(6)} %copy.7.pcount), custom_call_target="tpu_custom_call" | custom-call | flops 536870912 | bytes 65536 | tf_op jit(solution)/shard_map/vortex_pairs/pallas_call | solution.py:414
  46.1 1.5 %fusion = (f32[3,1024]{1,0:T(4,128)}, f32[3,1024]{1,0:T(4,128)}) fusion(f32[6,1024]{1,0:T(8,128)} %vortex_pairs.1), kind=kLoop, calls=%fused_computation | loop fusion | bytes 49152 | tf_op jit(solution)/shard_map/slice | solution.py:438

commit v5 on v4

--- a/solution.py
+++ b/solution.py
@@ -390,11 +390,17 @@
                 if e == d:
                     ahead[q].wait_send()
 
-    for cp in back_l + back_h:
+    for cp in back_l:
         cp.wait_recv()
     for q in range(NB):
-        pb[q] = ((hrecv[0, q] + hrecv[1, q]) + (hrecv[2, q] + hrecv[3, q])) + (
-            (lback[0, q] + lback[1, q]) + (lback[2, q] + lback[3, q]))
+        pa[q] = (lback[0, q] + lback[1, q]) + (lback[2, q] + lback[3, q])
+    for t in range(8):
+        lanes = slice(128 * t, 128 * t + 128)
+        sout[:, lanes] = sout[:, lanes] + pa[t // 2, pl.ds(t % 2, 6, stride=2), :]
+    for cp in back_h:
+        cp.wait_recv()
+    for q in range(NB):
+        pb[q] = (hrecv[0, q] + hrecv[1, q]) + (hrecv[2, q] + hrecv[3, q])
     for t in range(8):
         lanes = slice(128 * t, 128 * t + 128)
         result[:, lanes] = sout[:, lanes] + pb[t // 2, pl.ds(t % 2, 6, stride=2), :]

time: 47.8 us -> 47.8 us (level)
  no operation moved by 1% of the time
where the time goes in v5:
time: 47.8 us; the launch traced here: 47.5 us
  Pallas kernels  44.8 us (94%)
  local copies, waits for them, and re-layouts  1.45 us (3%)
  between operations  1.29 us (3%)
    pallas_call x1, Pallas kernels, local(): pl.pallas_call(kernel, out_shape=out, in_specs=[hbm, hbm, hbm, sm, sm], o...  44.8 us
    slice x1, local copies, waits for them, and re-layouts, local(): return (result[:3], result[3:])  1.45 us

profile of v5, /device:TPU:1, one launch (start us, length us, event | category | flops | bytes accessed | tf_op | source)
XLA Modules:
  0.0 47.5 jit_solution(15409735540014983648)
XLA Ops:
  1.3 44.8 %vortex_pairs.1 = f32[6,1024]{1,0:T(8,128)} custom-call(f32[3,1024]{1,0:T(4,128)} %pos_in.1, f32[3,1024]{1,0:T(4,128)} %stg_in.1, f32[8,128]{1,0:T(8,128)} %bitcast.1, s32[2,1,1,2]{3,2,1,0:T(1,128)} %plist.1, s32[1,1]{1,0:T(1,128)S(6)} %copy.7.pcount), custom_call_target="tpu_custom_call" | custom-call | flops 536870912 | bytes 65536 | tf_op jit(solution)/shard_map/vortex_pairs/pallas_call | solution.py:420
  46.1 1.5 %fusion = (f32[3,1024]{1,0:T(4,128)}, f32[3,1024]{1,0:T(4,128)}) fusion(f32[6,1024]{1,0:T(8,128)} %vortex_pairs.1), kind=kLoop, calls=%fused_computation | loop fusion | bytes 49152 | tf_op jit(solution)/shard_map/slice | solution.py:444
